TPU v7x, 512 devices: a whole 4x4x16 slice. The times are simulated.
512 devices in a mesh: row: 32 (over z, core), col: 16 (over x, y).
Axes of the slice: x: 4, y: 4, z: 16, core: 2. Of those that a mesh axis runs over, the one named last changes fastest.
Arguments:
- rhs: bfloat16 [3, 32, 64, 256], P(None, 'row'), may hold values from -6 to 6
- dinv: bfloat16 [3, 32, 256, 256], P(None, 'row'), as said below
- tiles: bfloat16 [2, 32, 32, 256, 256], P(None, 'row', 'col'), may hold values from -0.046875 to 0.046875
- pattern: int32 [2, 2, 32, 32], P(None, None, 'row', 'col'), may hold values from 0 to 31, as said below
Outputs:
- solution: float32 [3, 32, 64, 256], P(None, 'row')
Inputs may be any that keep to these rules, and one draw needn't show every extreme that they name: pattern[0, l, p, t] = p; pattern[1, l, p, t] = j has (j) modulo the size of col equal to t // 2; positions may repeat, and repeated tiles add. `dinv`: lower triangular with a positive diagonal.
All inputs are finite; a program needn't handle non-finite values.
Results may differ from a plain program's by a relative error of at most 0.0055.
Values may be sent and summed in bfloat16 or wider, within the bound.
A program may use at most 64 MiB of HBM per device.

v0:
```python
import jax
import jax.numpy as jnp
from jax import lax
from jax.sharding import PartitionSpec as P


def broadcast(block, axis, holder):
    block = jnp.where(lax.axis_index(axis) == holder, block, jnp.zeros_like(block))
    return lax.psum(block, axis)


def collect(rounded, mine_col, col_count, repeat):
    pieces = []
    for group in range(repeat):
        pieces.append(broadcast(rounded, "row", mine_col + col_count * group))
    return jnp.concatenate(pieces, 0)


def per_device(rhs, dinv, tiles, pattern):
    blocks = rhs.shape[1]
    levels_all = rhs.shape[0]
    col_count = lax.axis_size("col")
    row_count = lax.axis_size("row")
    repeat = row_count // col_count
    mine_row = lax.axis_index("row")
    mine_col = lax.axis_index("col")
    targets = pattern[0, :, 0, :] % blocks
    raw_cols = pattern[1, :, 0, :]
    sources = raw_cols // blocks // col_count * blocks + raw_cols % blocks
    row_pick = (targets[:, None, :] == jnp.arange(blocks, dtype=jnp.int32)[None, :, None]).astype(
        jnp.float32
    )
    col_pick = (
        sources[:, None, :] == jnp.arange(repeat * blocks, dtype=jnp.int32)[None, :, None]
    ).astype(jnp.float32)
    fronts = [rhs]
    forward_all = [[] for front in fronts]
    rounded_all = [None for front in fronts]
    for level_now in range(levels_all):
        front_index = 0
        front_level = fronts[front_index][level_now]
        current = front_level.astype(jnp.float32)
        if level_now > 0:
            nearby = collect(rounded_all[front_index], mine_col, col_count, repeat)
            source = jnp.take(nearby, sources[level_now - 1], axis=0)
            product = jnp.einsum(
                "sjb,sab->sja", source, tiles[level_now - 1, 0], preferred_element_type=jnp.float32
            )
            partial_value = jnp.sum(
                row_pick[level_now - 1][:, :, None, None] * product[None], axis=1
            )
            total_sum = lax.psum(partial_value, "col")
            current = current - total_sum
        solved = jnp.einsum(
            "rjb,rab->rja",
            current.astype(jnp.bfloat16),
            dinv[level_now],
            preferred_element_type=jnp.float32,
        )
        forward_all[front_index].append(solved)
        rounded_all[front_index] = solved.astype(jnp.bfloat16)
    backward_all = [[None] * levels_all for front in fronts]
    following_all = [None for front in fronts]
    for level_now in range(levels_all - 1, -1, -1):
        front_index = 0
        remainder = forward_all[front_index][level_now]
        if level_now < levels_all - 1:
            source = jnp.take(following_all[front_index], targets[level_now], axis=0)
            product = jnp.einsum(
                "sja,sab->sjb", source, tiles[level_now, 0], preferred_element_type=jnp.float32
            )
            partial_value = jnp.sum(col_pick[level_now][:, :, None, None] * product[None], axis=1)
            column_total = lax.psum(partial_value, "row")
            shaped = column_total.reshape((repeat, blocks) + column_total.shape[1:])
            picked = lax.dynamic_index_in_dim(shaped, mine_row // col_count, 0, keepdims=False)
            arrived = broadcast(picked, "col", mine_row % col_count)
            remainder = remainder - arrived
        solved = jnp.einsum(
            "rjb,rba->rja",
            remainder.astype(jnp.bfloat16),
            dinv[level_now],
            preferred_element_type=jnp.float32,
        )
        backward_all[front_index][level_now] = solved
        following_all[front_index] = solved.astype(jnp.bfloat16)
    front_index = 0
    levels_stack = jnp.stack(backward_all[front_index])
    return levels_stack


def solution(mesh):
    in_specs = (
        P(None, "row", None, None),
        P(None, "row", None, None),
        P(None, "row", "col", None, None),
        P(None, None, "row", "col"),
    )
    out_specs = P(None, "row", None, None)
    return jax.shard_map(
        per_device, mesh=mesh, in_specs=in_specs, out_specs=out_specs, check_vma=False
    )
```

profile of v0, /device:TPU:2, one launch (start us, length us, event | category | flops | bytes accessed | tf_op | source)
XLA Modules:
  0.0 1224.9 jit_solution(12864337464634439809)
XLA Ops:
  6.5 1.1 fusion.18
  8.4 0.7 slice.51
  9.2 188.0 %all-reduce.25.cloned.1.call-done = (bf16[1,64,256]{2,1,0:T(8,128)(2,1)}, bf16[1,64,256]{2,1,0:T(8,128)(2,1)}) async-done(((bf16[1,64,256]{2,1,0:T(8,128)(2,1)}, bf16[1,64,256]{2,1,0:T(8,128)(2,1)}), (bf16[1,64,256]{2,1,0:T(8,128)(2,1)}, bf16[1,64,256]{2,1,0:T(8,128)(2,1)})) %all-reduce.25.cloned.1.call-update) | async-done | bytes 65552 | tf_op jit(solution)/shard_map/psum | solution.py:9
  197.2 0.8 pad_maximum_fusion.1
  198.6 0.8 convolution_bitcast_fusion.2
  199.5 106.2 %all-reduce.11.cloned.1.call-done = f32[1,64,256]{2,1,0:T(8,128)} async-done(((f32[1,64,256]{2,1,0:T(8,128)}), f32[1,64,256]{2,1,0:T(8,128)}) %all-reduce.11.cloned.1.call-update) | async-done | bytes 65552 | tf_op jit(solution)/shard_map/psum | solution.py:52
  305.7 1.0 fusion.15
  306.7 0.7 select_bitcast_fusion.1
  307.4 183.7 %all-reduce.23.cloned.1.call-done = (bf16[1,64,256]{2,1,0:T(8,128)(2,1)}, bf16[1,64,256]{2,1,0:T(8,128)(2,1)}) async-done(((bf16[1,64,256]{2,1,0:T(8,128)(2,1)}, bf16[1,64,256]{2,1,0:T(8,128)(2,1)}), (bf16[1,64,256]{2,1,0:T(8,128)(2,1)}, bf16[1,64,256]{2,1,0:T(8,128)(2,1)})) %all-reduce.23.cloned.1.call-update) | async-done | bytes 65552 | tf_op jit(solution)/shard_map/psum | solution.py:9
  491.1 0.8 pad_maximum_fusion.2
  492.5 0.8 convolution_bitcast_fusion.1
  493.4 106.0 %all-reduce.13.cloned.1.call-done = f32[1,64,256]{2,1,0:T(8,128)} async-done(((f32[1,64,256]{2,1,0:T(8,128)}), f32[1,64,256]{2,1,0:T(8,128)}) %all-reduce.13.cloned.1.call-update) | async-done | bytes 65552 | tf_op jit(solution)/shard_map/psum | solution.py:52
  599.4 1.1 fusion.57
  600.8 0.7 multiply_reduce_fusion.1
  601.6 195.6 %all-reduce.15.cloned.1.call-done = f32[2,64,256]{2,1,0:T(8,128)} async-done(((f32[2,64,256]{2,1,0:T(8,128)}), f32[2,64,256]{2,1,0:T(8,128)}) %all-reduce.15.cloned.1.call-update) | async-done | bytes 131088 | tf_op jit(solution)/shard_map/psum | solution.py:73
  797.2 1.5 dynamic-slice_select_fusion.1
  798.7 109.0 %all-reduce.17.cloned.1.call-done = f32[1,64,256]{2,1,0:T(8,128)} async-done(((f32[1,64,256]{2,1,0:T(8,128)}), f32[1,64,256]{2,1,0:T(8,128)}) %all-reduce.17.cloned.1.call-update) | async-done | bytes 65552 | tf_op jit(solution)/shard_map/psum | solution.py:9
  907.8 1.0 fusion.62
  908.9 0.8 multiply_reduce_fusion
  909.8 195.9 %all-reduce.19.cloned.1.call-done = f32[2,64,256]{2,1,0:T(8,128)} async-done(((f32[2,64,256]{2,1,0:T(8,128)}), f32[2,64,256]{2,1,0:T(8,128)}) %all-reduce.19.cloned.1.call-update) | async-done | bytes 131088 | tf_op jit(solution)/shard_map/psum | solution.py:73
  1105.7 1.5 dynamic-slice_select_fusion
  1107.2 109.2 %all-reduce.21.cloned.1.call-done = f32[1,64,256]{2,1,0:T(8,128)} async-done(((f32[1,64,256]{2,1,0:T(8,128)}), f32[1,64,256]{2,1,0:T(8,128)}) %all-reduce.21.cloned.1.call-update) | async-done | bytes 65552 | tf_op jit(solution)/shard_map/psum | solution.py:9
  1216.4 1.0 convolution_bitcast_fusion
  1217.4 0.7 pad_maximum_fusion
  (33 shorter events, 2.6 us)
Async XLA Ops:
  6.5 192.0 %copy-start.1 = (bf16[2,1,2,256,256]{4,3,2,1,0:T(8,128)(2,1)S(1)}, bf16[2,1,2,256,256]{4,3,2,1,0:T(8,128)(2,1)}, u32[]{:S(2)}) copy-start(bf16[2,1,2,256,256]{4,3,2,1,0:T(8,128)(2,1)} %param.10) | copy-start | bytes 1572868
  6.5 190.7 %all-reduce.25.cloned.1.call-start = ((), (), s32[]{:S(2)}) async-start(), calls=%async_computation.7 | async-start | bytes 131072 | tf_op jit(solution)/shard_map/psum | solution.py:9
  8.4 297.3 %copy-start = (bf16[3,1,256,256]{3,2,1,0:T(8,128)(2,1)S(1)}, bf16[3,1,256,256]{3,2,1,0:T(8,128)(2,1)}, u32[]{:S(2)}) copy-start(bf16[3,1,256,256]{3,2,1,0:T(8,128)(2,1)} %param.9) | copy-start | bytes 1179652
  8.4 297.3 %all-reduce.11.cloned.1.call-start = ((), (), s32[]{:S(2)}) async-start(), calls=%async_computation | async-start | bytes 131072 | tf_op jit(solution)/shard_map/psum | solution.py:52
  198.6 107.1 %copy-start.2 = (bf16[3,1,64,256]{3,2,1,0:T(8,128)(2,1)S(1)}, bf16[3,1,64,256]{3,2,1,0:T(8,128)(2,1)}, u32[]{:S(2)}) copy-start(bf16[3,1,64,256]{3,2,1,0:T(8,128)(2,1)} %param.8) | copy-start | bytes 294916
  199.4 291.7 %all-reduce.23.cloned.1.call-start = ((), (), s32[]{:S(2)}) async-start(), calls=%async_computation.6 | async-start | bytes 131072 | tf_op jit(solution)/shard_map/psum | solution.py:9
  307.4 292.1 %all-reduce.13.cloned.1.call-start = ((), (), s32[]{:S(2)}) async-start(), calls=%async_computation.1 | async-start | bytes 131072 | tf_op jit(solution)/shard_map/psum | solution.py:52
  493.4 303.8 %all-reduce.15.cloned.1.call-start = ((), (), s32[]{:S(2)}) async-start(), calls=%async_computation.2 | async-start | bytes 262144 | tf_op jit(solution)/shard_map/psum | solution.py:73
  601.5 306.3 %all-reduce.17.cloned.1.call-start = ((), (), s32[]{:S(2)}) async-start(), calls=%async_computation.3 | async-start | bytes 131072 | tf_op jit(solution)/shard_map/psum | solution.py:9
  798.7 307.0 %all-reduce.19.cloned.1.call-start = ((), (), s32[]{:S(2)}) async-start(), calls=%async_computation.4 | async-start | bytes 262144 | tf_op jit(solution)/shard_map/psum | solution.py:73
  909.7 306.7 %all-reduce.21.cloned.1.call-start = ((), (), s32[]{:S(2)}) async-start(), calls=%async_computation.5 | async-start | bytes 131072 | tf_op jit(solution)/shard_map/psum | solution.py:9
Sparse Core Ops, SparseCore 0:
  9.8 187.3 all-reduce.24
  200.7 104.9 all-reduce.10
  308.1 182.9 all-reduce.22
  494.5 104.8 all-reduce.12
  601.7 195.4 all-reduce.14
  800.6 107.1 all-reduce.16
  910.1 195.4 all-reduce.18
  1109.2 107.1 all-reduce.20
where the time goes:
time: 1230 us; the launch traced here: 1220 us
  waiting for transfers between devices  1190 us (97%)
  between operations  13.6 us (1%)
    psum x4, waiting for transfers between devices, broadcast(): return lax.psum(block, axis)  590 us
    psum x2, waiting for transfers between devices, per_device(): column_total = lax.psum(partial_value, 'row')  391 us
    psum x2, waiting for transfers between devices, per_device(): total_sum = lax.psum(partial_value, 'col')  212 us
  transfers between devices with their start and end apart: 8, of which 8 were waited for; matrix products, arithmetic and copies ran while one was open for 0% of the time, Pallas kernels for 0%

commit v1 on v0

--- a/solution.py
+++ b/solution.py
@@ -49,7 +49,7 @@
             partial_value = jnp.sum(
                 row_pick[level_now - 1][:, :, None, None] * product[None], axis=1
             )
-            total_sum = lax.psum(partial_value, "col")
+            total_sum = jnp.sum(lax.all_gather(partial_value, "col"), axis=0)
             current = current - total_sum
         solved = jnp.einsum(
             "rjb,rab->rja",

time: 1230 us -> 1120 us (0.911)
  waiting for transfers between devices: 1190 us -> 1090 us
    psum x2 -> x0, waiting for transfers between devices: 212 us -> none  [per_device(): total_sum = lax.psum(partial_value, 'col')]
    all_gather x0 -> x2, waiting for transfers between devices: none -> 104 us  [per_device(): total_sum = jnp.sum(lax.all_gather(partial_value, 'col'), axis=0)]
where the time goes in v1:
time: 1120 us
  waiting for transfers between devices  1090 us (97%)
  between operations  13.6 us (1%)
    psum x4, waiting for transfers between devices, broadcast(): return lax.psum(block, axis)  590 us
    psum x2, waiting for transfers between devices, per_device(): column_total = lax.psum(partial_value, 'row')  391 us
    all_gather x2, waiting for transfers between devices, per_device(): total_sum = jnp.sum(lax.all_gather(partial_value, 'col'), axis=0)  104 us
  transfers between devices with their start and end apart: 8, of which 8 were waited for; matrix products, arithmetic and copies ran while one was open for 0% of the time, Pallas kernels for 0%

profile of v1, /device:TPU:2, one launch (start us, length us, event | category | flops | bytes accessed | tf_op | source)
XLA Modules:
  0.0 1117.3 jit_solution(395398026023259927)
XLA Ops:
  6.5 1.1 fusion.18
  8.4 0.7 slice.51
  9.1 188.1 %all-reduce.19.cloned.1.call-done = (bf16[1,64,256]{2,1,0:T(8,128)(2,1)}, bf16[1,64,256]{2,1,0:T(8,128)(2,1)}) async-done(((bf16[1,64,256]{2,1,0:T(8,128)(2,1)}, bf16[1,64,256]{2,1,0:T(8,128)(2,1)}), (bf16[1,64,256]{2,1,0:T(8,128)(2,1)}, bf16[1,64,256]{2,1,0:T(8,128)(2,1)})) %all-reduce.19.cloned.1.call-update) | async-done | bytes 65552 | tf_op jit(solution)/shard_map/psum | solution.py:9
  197.2 0.8 pad_maximum_fusion.1
  198.6 0.8 convolution_bitcast_fusion.2
  199.5 52.4 %all-gather.5.cloned.1.call-done = f32[1024,256]{1,0:T(8,128)} async-done(((f32[64,256]{1,0:T(8,128)}), f32[1024,256]{1,0:T(8,128)}) %all-gather.5.cloned.1.call-update) | async-done | bytes 1048592 | tf_op jit(solution)/shard_map/all_gather | solution.py:52
  251.8 1.3 reduce.6
  253.3 0.7 select_bitcast_fusion.1
  254.1 183.3 %all-reduce.17.cloned.1.call-done = (bf16[1,64,256]{2,1,0:T(8,128)(2,1)}, bf16[1,64,256]{2,1,0:T(8,128)(2,1)}) async-done(((bf16[1,64,256]{2,1,0:T(8,128)(2,1)}, bf16[1,64,256]{2,1,0:T(8,128)(2,1)}), (bf16[1,64,256]{2,1,0:T(8,128)(2,1)}, bf16[1,64,256]{2,1,0:T(8,128)(2,1)})) %all-reduce.17.cloned.1.call-update) | async-done | bytes 65552 | tf_op jit(solution)/shard_map/psum | solution.py:9
  437.4 0.8 pad_maximum_fusion.2
  438.7 0.8 convolution_bitcast_fusion.1
  439.7 51.8 %all-gather.7.cloned.1.call-done = f32[1024,256]{1,0:T(8,128)} async-done(((f32[64,256]{1,0:T(8,128)}), f32[1024,256]{1,0:T(8,128)}) %all-gather.7.cloned.1.call-update) | async-done | bytes 1048592 | tf_op jit(solution)/shard_map/all_gather | solution.py:52
  491.4 1.3 reduce.7
  493.2 0.8 multiply_reduce_fusion.1
  494.1 195.6 %all-reduce.9.cloned.1.call-done = f32[2,64,256]{2,1,0:T(8,128)} async-done(((f32[2,64,256]{2,1,0:T(8,128)}), f32[2,64,256]{2,1,0:T(8,128)}) %all-reduce.9.cloned.1.call-update) | async-done | bytes 131088 | tf_op jit(solution)/shard_map/psum | solution.py:73
  689.6 1.5 dynamic-slice_select_fusion.1
  691.2 109.0 %all-reduce.11.cloned.1.call-done = f32[1,64,256]{2,1,0:T(8,128)} async-done(((f32[1,64,256]{2,1,0:T(8,128)}), f32[1,64,256]{2,1,0:T(8,128)}) %all-reduce.11.cloned.1.call-update) | async-done | bytes 65552 | tf_op jit(solution)/shard_map/psum | solution.py:9
  800.2 1.0 fusion.59
  801.4 0.8 multiply_reduce_fusion
  802.2 195.9 %all-reduce.13.cloned.1.call-done = f32[2,64,256]{2,1,0:T(8,128)} async-done(((f32[2,64,256]{2,1,0:T(8,128)}), f32[2,64,256]{2,1,0:T(8,128)}) %all-reduce.13.cloned.1.call-update) | async-done | bytes 131088 | tf_op jit(solution)/shard_map/psum | solution.py:73
  998.1 1.5 dynamic-slice_select_fusion
  999.6 109.2 %all-reduce.15.cloned.1.call-done = f32[1,64,256]{2,1,0:T(8,128)} async-done(((f32[1,64,256]{2,1,0:T(8,128)}), f32[1,64,256]{2,1,0:T(8,128)}) %all-reduce.15.cloned.1.call-update) | async-done | bytes 65552 | tf_op jit(solution)/shard_map/psum | solution.py:9
  1108.8 1.0 convolution_bitcast_fusion
  1109.8 0.7 pad_maximum_fusion
  (35 shorter events, 3.0 us)
Async XLA Ops:
  6.5 192.0 %copy-start.1 = (bf16[2,1,2,256,256]{4,3,2,1,0:T(8,128)(2,1)S(1)}, bf16[2,1,2,256,256]{4,3,2,1,0:T(8,128)(2,1)}, u32[]{:S(2)}) copy-start(bf16[2,1,2,256,256]{4,3,2,1,0:T(8,128)(2,1)} %param.10) | copy-start | bytes 1572868
  6.5 190.7 %all-reduce.19.cloned.1.call-start = ((), (), s32[]{:S(2)}) async-start(), calls=%async_computation.7 | async-start | bytes 131072 | tf_op jit(solution)/shard_map/psum | solution.py:9
  8.4 243.5 %all-gather.5.cloned.1.call-start = ((), (), s32[]{:S(2)}) async-start(), calls=%async_computation.4 | async-start | bytes 1114112 | tf_op jit(solution)/shard_map/all_gather | solution.py:52
  199.4 238.0 %all-reduce.17.cloned.1.call-start = ((), (), s32[]{:S(2)}) async-start(), calls=%async_computation.6 | async-start | bytes 131072 | tf_op jit(solution)/shard_map/psum | solution.py:9
  251.8 1.4 copy-start
  251.8 1.4 copy-start.2
  254.0 237.4 %all-gather.7.cloned.1.call-start = ((), (), s32[]{:S(2)}) async-start(), calls=%async_computation.5 | async-start | bytes 1114112 | tf_op jit(solution)/shard_map/all_gather | solution.py:52
  439.6 250.0 %all-reduce.9.cloned.1.call-start = ((), (), s32[]{:S(2)}) async-start(), calls=%async_computation | async-start | bytes 262144 | tf_op jit(solution)/shard_map/psum | solution.py:73
  494.0 306.2 %all-reduce.11.cloned.1.call-start = ((), (), s32[]{:S(2)}) async-start(), calls=%async_computation.1 | async-start | bytes 131072 | tf_op jit(solution)/shard_map/psum | solution.py:9
  691.1 307.0 %all-reduce.13.cloned.1.call-start = ((), (), s32[]{:S(2)}) async-start(), calls=%async_computation.2 | async-start | bytes 262144 | tf_op jit(solution)/shard_map/psum | solution.py:73
  802.2 306.7 %all-reduce.15.cloned.1.call-start = ((), (), s32[]{:S(2)}) async-start(), calls=%async_computation.3 | async-start | bytes 131072 | tf_op jit(solution)/shard_map/psum | solution.py:9
Sparse Core Ops, SparseCore 0:
  9.8 187.3 all-reduce.18
  200.7 51.1 all-gather.4
  254.4 182.9 all-reduce.16
  440.3 51.1 all-gather.6
  494.1 195.4 all-reduce.8
  693.0 107.1 all-reduce.10
  802.5 195.4 all-reduce.12
  1001.6 107.1 all-reduce.14
